TPU v7x, 256 devices: a whole 4x4x8 slice. The times are simulated.
256 devices in a mesh: section: 16 (over z, core), tensor: 16 (over y, x).
Axes of the slice: x: 4, y: 4, z: 8, core: 2. Of those that a mesh axis runs over, the one named last changes fastest.
Arguments:
- teacher_hidden: bfloat16 [640, 8192], P('tensor', 'section'), may hold values from -6 to 6
- student_hidden: bfloat16 [640, 4096], P('tensor', 'section'), may hold values from -6 to 6
- teacher_head: bfloat16 [8192, 65536], P('section', 'tensor'), may hold values from -0.143631065 to 0.143631065
- student_head: bfloat16 [4096, 65536], P('section', 'tensor'), may hold values from -0.203125 to 0.203125
- targets: int32 [640], P('section'), may hold values from 0 to 65535
Outputs:
- loss: float32 [], replicated
- grad_hidden: bfloat16 [640, 4096], P('tensor', 'section')
- grad_head: bfloat16 [4096, 65536], P('section', 'tensor')
All inputs are finite; a program needn't handle non-finite values.
Results may differ from a plain program's by a relative error of at most 0.0034.
Values may be sent and summed in bfloat16 or wider, within the bound.
No kernel may reach another device: no remote copies, remote signals or barrier semaphores. Data moves between devices by JAX's collectives and lax.ppermute only.
A program may use at most 128 MiB of HBM per device.

v0:
```python
import jax
import jax.numpy as jnp
from jax import lax
from jax.sharding import PartitionSpec as P

tau = 2.0


def shards(teacher_hidden, student_hidden, teacher_head, student_head, targets):
    teacher_all, student_all = (
        lax.all_gather(teacher_hidden, "tensor", axis=0, tiled=True),
        lax.all_gather(student_hidden, "tensor", axis=0, tiled=True),
    )
    tok_block = targets.shape[0]
    voc_local = teacher_head.shape[1]
    rows = teacher_all
    teacher_logits = lax.psum_scatter(
        jnp.dot(rows, teacher_head, preferred_element_type=jnp.float32),
        "section",
        scatter_dimension=0,
        tiled=True,
    )
    rows = student_all
    student_logits = lax.psum_scatter(
        jnp.dot(rows, student_head, preferred_element_type=jnp.float32),
        "section",
        scatter_dimension=0,
        tiled=True,
    )
    teacher_max, student_max = lax.pmax(
        (jnp.max(teacher_logits, axis=1), jnp.max(student_logits, axis=1)), "tensor"
    )
    offset = lax.axis_index("tensor") * voc_local
    column_ids = offset + lax.broadcasted_iota(jnp.int32, (tok_block, voc_local), 1)
    onehot = (column_ids == targets[:, None]).astype(jnp.float32)
    p_terms = jnp.exp((teacher_logits - teacher_max[:, None]) / tau)
    q_terms = jnp.exp((student_logits - student_max[:, None]) / tau)
    s_terms = jnp.exp(student_logits - student_max[:, None])
    p_total, q_total, s_total, cross, picked = lax.psum(
        (
            jnp.sum(p_terms, axis=1),
            jnp.sum(q_terms, axis=1),
            jnp.sum(s_terms, axis=1),
            jnp.sum(p_terms * (teacher_logits - student_logits), axis=1),
            jnp.sum(onehot * student_logits, axis=1),
        ),
        "tensor",
    )
    kl_rows = (
        cross / (tau * p_total)
        - (teacher_max - student_max) / tau
        - jnp.log(p_total)
        + jnp.log(q_total)
    )
    row_loss = tau * tau * kl_rows + student_max + jnp.log(s_total) - picked
    loss = lax.psum(jnp.sum(row_loss), "section") / (tok_block * lax.axis_size("section"))
    p_prob = p_terms / p_total[:, None]
    q_prob = q_terms / q_total[:, None]
    s_prob = s_terms / s_total[:, None]
    logit_grad = (tau * (q_prob - p_prob) + s_prob - onehot).astype(jnp.bfloat16)
    piece = lax.all_gather(logit_grad, "section", axis=0, tiled=True)
    rows = student_all
    head_acc = lax.dot_general(
        rows, piece, (((0,), (0,)), ((), ())), preferred_element_type=jnp.float32
    )
    partial_rows = lax.dot_general(
        piece, student_head, (((1,), (1,)), ((), ())), preferred_element_type=jnp.float32
    )
    grad_hidden = lax.psum_scatter(partial_rows, "tensor", scatter_dimension=0, tiled=True).astype(
        jnp.bfloat16
    )
    return (loss, grad_hidden, head_acc.astype(jnp.bfloat16))


def solution(mesh):
    placed = (
        P("tensor", "section"),
        P("tensor", "section"),
        P("section", "tensor"),
        P("section", "tensor"),
        P("section"),
    )
    return jax.shard_map(
        shards,
        mesh=mesh,
        in_specs=placed,
        out_specs=(P(), P("tensor", "section"), P("section", "tensor")),
        check_vma=False,
    )
```

profile of v0, /device:TPU:2, one launch (start us, length us, event | category | flops | bytes accessed | tf_op | source)
XLA Modules:
  0.0 402.8 jit_solution(17284586410088657765)
XLA Ops:
  7.2 0.0 copy-start
  7.2 0.0 reduce-scatter.6.cloned.1.call-start
  7.2 24.3 %all_gather.9 = bf16[640,512]{1,0:T(8,128)(2,1)S(1)} all-gather(bf16[40,512]{1,0:T(8,128)(2,1)} %param.5), channel_id=1, replica_groups=mesh['section'=16,'tensor'=16] {'tensor'}, dimensions={0}, use_global_device_ids=true | all-gather | bytes 696320 | tf_op jit(solution)/shard_map/all_gather | solution.py:11
  31.5 7.7 %fusion.6 = f32[640,4096]{1,0:T(8,128)} fusion(bf16[640,512]{1,0:T(8,128)(2,1)S(1)} %all_gather.9, bf16[512,4096]{1,0:T(8,128)(2,1)} %param.7), kind=kOutput, calls=%fused_computation.15 | convolution fusion | flops 2684354560 | bytes 15335424 | tf_op jit(solution)/shard_map/dot_general | solution.py:18
  39.2 0.0 copy-start.1
  39.2 0.0 reduce-scatter.6.cloned.1.call-update
  39.2 0.0 reduce-scatter.8.cloned.1.call-start
  39.3 0.7 copy-done.1
  39.9 22.2 %all_gather.10 = bf16[640,256]{1,0:T(8,128)(2,1)S(1)} all-gather(bf16[40,256]{1,0:T(8,128)(2,1)S(1)} %copy-done.1), channel_id=1, replica_groups=mesh['section'=16,'tensor'=16] {'tensor'}, dimensions={0}, use_global_device_ids=true | all-gather | bytes 348160 | tf_op jit(solution)/shard_map/all_gather | solution.py:12
  62.1 0.0 copy-done
  62.1 5.4 %fusion.7 = f32[640,4096]{1,0:T(8,128)} fusion(bf16[640,256]{1,0:T(8,128)(2,1)S(1)} %all_gather.10, bf16[256,4096]{1,0:T(8,128)(2,1)S(1)} %copy-done), kind=kOutput, calls=%fused_computation.16 | convolution fusion | flops 1342177280 | bytes 12910592 | tf_op jit(solution)/shard_map/dot_general | solution.py:25
  67.5 0.0 copy-start.2
  67.5 0.0 reduce-scatter.8.cloned.1.call-update
  67.5 0.0 all-gather.2.cloned.1.call-start
  67.6 47.6 %reduce-scatter.6.cloned.1.call-done = f32[40,4096]{1,0:T(8,128)} async-done(((f32[640,4096]{1,0:T(8,128)}), f32[40,4096]{1,0:T(8,128)}) %reduce-scatter.6.cloned.1.call-update) | async-done | bytes 655376 | tf_op jit(solution)/shard_map/reduce_scatter | solution.py:17
  115.2 1.2 reduce_max.18
  116.4 75.4 %reduce-scatter.8.cloned.1.call-done = f32[40,4096]{1,0:T(8,128)} async-done(((f32[640,4096]{1,0:T(8,128)}), f32[40,4096]{1,0:T(8,128)}) %reduce-scatter.8.cloned.1.call-update) | async-done | bytes 655376 | tf_op jit(solution)/shard_map/reduce_scatter | solution.py:24
  191.8 1.2 reduce_max.19
  193.0 36.5 %all-reduce.2 = (f32[40]{0:T(128)S(1)}, f32[40]{0:T(128)S(1)}) all-reduce(f32[40]{0:T(128)S(1)} %reduce_max.18, f32[40]{0:T(128)S(1)} %reduce_max.19), channel_id=1, replica_groups=mesh['section'=16,'tensor'=16] {'tensor'}, use_global_device_ids=true, to_apply=%region_2.0 | all-reduce | flops 80 | bytes 640 | tf_op jit(solution)/shard_map/pmax | solution.py:30
  229.5 0.0 copy-done.2
  229.5 1.9 multiply_reduce_fusion
  231.4 39.9 %all-reduce.1 = (f32[40]{0:T(128)S(1)}, f32[40]{0:T(128)S(1)}, f32[40]{0:T(128)S(1)}, f32[40]{0:T(128)S(1)}, f32[40]{0:T(128)S(1)}) all-reduce(f32[40]{0:T(128)S(1)} %get-tuple-element.13, f32[40]{0:T(128)S(1)} %get-tuple-element.14, f32[40]{0:T(128)S(1)} %get-tuple-element.15, ...), channel_id=1, replica_groups=mesh['section'=16,'tensor'=16] {'tensor'}, use_global_device_ids=true, to_apply=%region_15.0 | all-reduce | flops 200 | bytes 1600 | tf_op jit(solution)/shard_map/psum | solution.py:39
  271.4 2.5 fusion.3
  273.9 0.0 all-gather.2.cloned.1.call-update
  273.9 0.0 reduce-scatter.10.cloned.1.call-start
  274.0 38.9 %all-gather.2.cloned.1.call-done = bf16[640,4096]{1,0:T(8,128)(2,1)} async-done(((bf16[40,4096]{1,0:T(8,128)(2,1)}), bf16[640,4096]{1,0:T(8,128)(2,1)}) %all-gather.2.cloned.1.call-update) | async-done | bytes 5242896 | tf_op jit(solution)/shard_map/all_gather | solution.py:61
  312.8 4.9 %fusion.8 = f32[640,256]{1,0:T(8,128)} fusion(bf16[640,4096]{1,0:T(8,128)(2,1)} %all-gather.2.cloned.1.call-done, bf16[256,4096]{1,0:T(8,128)(2,1)S(1)} %copy-done), kind=kOutput, calls=%fused_computation.17 | convolution fusion | flops 1342177280 | bytes 7995392 | tf_op jit(solution)/shard_map/dot_general | solution.py:66
  317.7 0.0 reduce-scatter.10.cloned.1.call-update
  317.7 0.6 subtract_reduce_fusion
  318.3 26.3 %psum.47 = f32[]{:T(128)} all-reduce(f32[]{:T(128)} %subtract_reduce_fusion), channel_id=1, replica_groups=mesh['section'=16,'tensor'=16] {'section'}, use_global_device_ids=true, to_apply=%region_17.0 | all-reduce | flops 1 | bytes 8 | tf_op jit(solution)/shard_map/psum | solution.py:56
  345.2 5.7 %fusion = bf16[256,4096]{0,1:T(8,128)(2,1)} fusion(bf16[640,4096]{1,0:T(8,128)(2,1)} %all-gather.2.cloned.1.call-done, bf16[640,256]{1,0:T(8,128)(2,1)S(1)} %all_gather.10), kind=kOutput, calls=%fused_computation.1 | convolution fusion | flops 1343225856 | bytes 7667712 | tf_op jit(solution)/shard_map/dot_general | solution.py:63
  351.0 4.1 %copy.9 = bf16[256,4096]{1,0:T(8,128)(2,1)} copy(bf16[256,4096]{0,1:T(8,128)(2,1)} %fusion) | data formatting | bytes 4194304
  355.1 38.7 %reduce-scatter.10.cloned.1.call-done = f32[40,256]{1,0:T(8,128)} async-done(((f32[640,256]{1,0:T(8,128)}), f32[40,256]{1,0:T(8,128)}) %reduce-scatter.10.cloned.1.call-update) | async-done | bytes 40976
  393.8 1.4 convert_element_type.17
  (1 shorter events, 0.0 us)
Async XLA Ops:
  7.2 55.0 %copy-start = (bf16[256,4096]{1,0:T(8,128)(2,1)S(1)}, bf16[256,4096]{1,0:T(8,128)(2,1)}, u32[]{:S(2)}) copy-start(bf16[256,4096]{1,0:T(8,128)(2,1)} %param.8) | copy-start | bytes 6291460
  7.2 108.0 %reduce-scatter.6.cloned.1.call-start = ((), (), s32[]{:S(2)}) async-start(), calls=%async_computation.3 | async-start | bytes 11141120 | tf_op jit(solution)/shard_map/reduce_scatter | solution.py:17
  39.2 0.7 copy-start.1
  39.2 152.5 %reduce-scatter.8.cloned.1.call-start = ((), (), s32[]{:S(2)}) async-start(), calls=%async_computation.4 | async-start | bytes 11141120 | tf_op jit(solution)/shard_map/reduce_scatter | solution.py:24
  67.5 162.0 %copy-start.2 = (s32[40]{0:T(128)S(1)}, s32[40]{0:T(128)}, u32[]{:S(2)}) copy-start(s32[40]{0:T(128)} %param.9) | copy-start | bytes 484
  67.5 245.3 %all-gather.2.cloned.1.call-start = ((), (), s32[]{:S(2)}) async-start(), calls=%async_computation.5 | async-start | bytes 5570560 | tf_op jit(solution)/shard_map/all_gather | solution.py:61
  273.9 119.9 %reduce-scatter.10.cloned.1.call-start = ((), (), s32[]{:S(2)}) async-start(), calls=%async_computation.6 | async-start | bytes 696320
Sparse Core Ops, SparseCore 0:
  39.4 75.7 reduce-scatter.5
  117.7 74.0 reduce-scatter.7
  274.0 38.7 all-gather.1
  317.8 75.9 reduce-scatter.9
where the time goes:
time: 404 us; the launch traced here: 403 us
  waiting for transfers between devices  201 us (50%)
  blocking collectives  149 us (37%)
  matrix products  23.7 us (6%)
  between operations  15.6 us (4%)
  other arithmetic  8.9 us (2%)
  local copies, waits for them, and re-layouts  4.74 us (1%)
    reduce_scatter x1, waiting for transfers between devices, shards(): lax.psum_scatter(jnp.dot(rows, student_head, preferred_element_type=jnp.f...  75.4 us
    reduce_scatter x1, waiting for transfers between devices, shards(): lax.psum_scatter(jnp.dot(rows, teacher_head, preferred_element_type=jnp.f...  47.6 us
    psum x1, blocking collectives, shards(): lax.psum((jnp.sum(p_terms, axis=1), jnp.sum(q_terms, axis=1), jnp.sum(s_t...  39.9 us
    all_gather x1, waiting for transfers between devices, shards(): piece = lax.all_gather(logit_grad, 'section', axis=0, tiled=True)  38.9 us
    unnamed x5, waiting for transfers between devices  38.8 us
    pmax x1, blocking collectives, shards(): lax.pmax((jnp.max(teacher_logits, axis=1), jnp.max(student_logits, axis=1...  36.5 us
    psum x1, blocking collectives, shards(): lax.psum(jnp.sum(row_loss), 'section')  26.3 us
    all_gather x1, blocking collectives, shards(): lax.all_gather(teacher_hidden, 'tensor', axis=0, tiled=True)  24.3 us
  transfers between devices with their start and end apart: 4, of which 4 were waited for; matrix products, arithmetic and copies ran while one was open for 4% of the time, Pallas kernels for 0%

commit v1 on v0

v1 whole, which is shorter than its diff:
```python
import jax
import jax.numpy as jnp
from jax import lax
from jax.sharding import PartitionSpec as P

tau = 2.0
f32 = jnp.float32
bf16 = jnp.bfloat16


def shards(teacher_hidden, student_hidden, teacher_head, student_head, targets):
    tensor_size = lax.axis_size("tensor")
    section_size = lax.axis_size("section")
    chips = section_size // 2
    half_way = chips // 2
    me = lax.axis_index("section")
    z, core = me // 2, me % 2
    tok_block, dt = teacher_hidden.shape
    ds = student_hidden.shape[1]
    voc_local = teacher_head.shape[1]
    half = voc_local // 2

    def along(x, step):
        perm = [
            (s, ((s // 2 + step) % chips) * 2 + s % 2) for s in range(section_size)
        ]
        return lax.ppermute(x, "section", perm)

    def swap(x):
        return lax.ppermute(x, "section", [(s, s ^ 1) for s in range(section_size)])

    def spread(x, axis):
        n = lax.axis_size(axis)
        return lax.all_to_all(
            jnp.broadcast_to(x[None], (n,) + x.shape), axis, 0, 0
        )

    student_head_sib = swap(student_head)
    teacher_head_sib = swap(teacher_head)
    hidden = spread(jnp.concatenate([teacher_hidden, student_hidden], axis=1), "tensor")

    def rolled(x, which):
        pair = x.reshape((chips, 2) + x.shape[1:])
        twice = jnp.concatenate([pair, pair], axis=0)
        out = lax.dynamic_slice(
            twice, (z, which, 0, 0), (chips, 1) + x.shape[1:]
        )
        return out.reshape((chips * x.shape[1],) + x.shape[2:])

    mine = rolled(hidden, core)
    others = rolled(hidden, 1 - core)
    mine_sib = swap(others)

    def logits_part(own, own_head, sib, sib_head):
        out = jnp.dot(own, own_head, preferred_element_type=f32) + jnp.dot(
            sib, sib_head, preferred_element_type=f32
        )
        return out.reshape(chips, tok_block, voc_local)

    student_part = logits_part(
        mine[:, dt:], student_head, mine_sib[:, dt:], student_head_sib
    )
    teacher_part = logits_part(
        mine[:, :dt], teacher_head, mine_sib[:, :dt], teacher_head_sib
    )

    def ring(part):
        right = along(part[half_way][:, :half], 1)
        left = along(part[half_way][:, half:], -1)
        for hop in range(1, half_way):
            mine_r, mine_l = part[half_way - hop], part[half_way + hop]
            if hop == 1:
                right = jnp.concatenate([right + mine_r[:, :half], mine_r[:, half:]], 1)
                left = jnp.concatenate([mine_l[:, :half], left + mine_l[:, half:]], 1)
            else:
                right = right + mine_r
                left = left + mine_l
            right, left = along(right, 1), along(left, -1)
        return part[0] + right + left

    student_logits = ring(student_part)
    teacher_logits = ring(teacher_part)

    offset = lax.axis_index("tensor") * voc_local
    column_ids = offset + lax.broadcasted_iota(jnp.int32, (tok_block, voc_local), 1)
    onehot = (column_ids == targets[:, None]).astype(f32)
    t_max = jnp.max(teacher_logits, axis=1)
    s_max = jnp.max(student_logits, axis=1)
    p_terms = jnp.exp((teacher_logits - t_max[:, None]) / tau)
    q_terms = jnp.exp((student_logits - s_max[:, None]) / tau)
    s_terms = jnp.exp(student_logits - s_max[:, None])
    stats = jnp.stack(
        [
            t_max,
            s_max,
            jnp.sum(p_terms, axis=1),
            jnp.sum(q_terms, axis=1),
            jnp.sum(s_terms, axis=1),
            jnp.sum(p_terms * (teacher_logits - student_logits), axis=1),
            jnp.sum(onehot * student_logits, axis=1),
            jnp.zeros_like(t_max),
        ]
    )
    every = spread(stats, "tensor")
    teacher_max = jnp.max(every[:, 0], axis=0)
    student_max = jnp.max(every[:, 1], axis=0)
    t_weight = jnp.exp((every[:, 0] - teacher_max) / tau)
    q_weight = jnp.exp((every[:, 1] - student_max) / tau)
    s_weight = jnp.exp(every[:, 1] - student_max)
    p_total = jnp.sum(t_weight * every[:, 2], axis=0)
    q_total = jnp.sum(q_weight * every[:, 3], axis=0)
    s_total = jnp.sum(s_weight * every[:, 4], axis=0)
    cross = jnp.sum(t_weight * every[:, 5], axis=0)
    picked = jnp.sum(every[:, 6], axis=0)
    kl_rows = (
        cross / (tau * p_total)
        - (teacher_max - student_max) / tau
        - jnp.log(p_total)
        + jnp.log(q_total)
    )
    row_loss = tau * tau * kl_rows + student_max + jnp.log(s_total) - picked

    p_prob = jnp.exp((teacher_logits - teacher_max[:, None]) / tau) / p_total[:, None]
    q_prob = jnp.exp((student_logits - student_max[:, None]) / tau) / q_total[:, None]
    s_prob = jnp.exp(student_logits - student_max[:, None]) / s_total[:, None]
    grad = (tau * (q_prob - p_prob) + s_prob - onehot).astype(bf16)

    pieces = [None] * chips
    pieces[0] = grad
    right = left = grad
    for hop in range(1, half_way):
        right, left = along(right, 1), along(left, -1)
        pieces[chips - hop], pieces[hop] = right, left
    pieces[half_way] = jnp.concatenate(
        [along(right[:, :half], 1), along(left[:, half:], -1)], axis=1
    )
    lg = jnp.concatenate(pieces, axis=0)
    lg_sib = swap(lg)

    loss_parts = spread(jnp.full((8, 128), jnp.sum(row_loss), f32), "section")
    loss = jnp.sum(loss_parts[:, 0, 0]) / (tok_block * section_size)

    def back(x):
        return lax.dot_general(
            x, student_head, (((1,), (1,)), ((), ())), preferred_element_type=f32
        ).reshape(chips, 1, tok_block, ds)

    rows_own, rows_sib = back(lg), back(lg_sib)
    rows = jnp.where(
        core == 0,
        jnp.concatenate([rows_own, rows_sib], axis=1),
        jnp.concatenate([rows_sib, rows_own], axis=1),
    )
    rows = jnp.concatenate([rows, rows], axis=0)
    rows = lax.dynamic_slice(
        rows, ((chips - z) % chips, 0, 0, 0), (chips, 2, tok_block, ds)
    ).reshape(tensor_size, tok_block, ds)
    grad_hidden = jnp.sum(lax.all_to_all(rows, "tensor", 0, 0), axis=0).astype(bf16)

    def outer(x, g):
        return lax.dot_general(
            x, g, (((0,), (0,)), ((), ())), preferred_element_type=f32
        )

    grad_head = (outer(mine[:, dt:], lg) + outer(others[:, dt:], lg_sib)).astype(bf16)
    return loss, grad_hidden, grad_head


def solution(mesh):
    placed = (
        P("tensor", "section"),
        P("tensor", "section"),
        P("section", "tensor"),
        P("section", "tensor"),
        P("section"),
    )
    return jax.shard_map(
        shards,
        mesh=mesh,
        in_specs=placed,
        out_specs=(P(), P("tensor", "section"), P("section", "tensor")),
        check_vma=False,
    )
```

time: 404 us -> 246 us (0.61)
  blocking collectives: 149 us -> 10.7 us
  waiting for transfers between devices: 201 us -> 135 us
  starting transfers between devices: 0.16 us -> 52.3 us
  between operations: 15.6 us -> 2.77 us
  other arithmetic: 8.9 us -> 13.5 us
    reduce_scatter x2 -> x0, waiting for transfers between devices: 123 us -> none  [the longest x1 75.4 us: shards(): lax.psum_scatter(jnp.dot(rows, student_head, preferred_element_type=jnp.f...]
    ppermute x0 -> x28, waiting for transfers between devices: none -> 106 us  [the longest x24 106 us: along(): return lax.ppermute(x, 'section', perm)]
    psum x2 -> x0, blocking collectives: 66.2 us -> none  [the longest x1 39.9 us: shards(): lax.psum((jnp.sum(p_terms, axis=1), jnp.sum(q_terms, axis=1), jnp.sum(s_t...]
    all_gather x2 -> x0, blocking collectives: 46.5 us -> none  [the longest x1 24.3 us: shards(): lax.all_gather(teacher_hidden, 'tensor', axis=0, tiled=True)]
    all_gather x1 -> x0, waiting for transfers between devices: 38.9 us -> none  [shards(): piece = lax.all_gather(logit_grad, 'section', axis=0, tiled=True)]
    unnamed x5 -> x0, waiting for transfers between devices: 38.8 us -> none
    pmax x1 -> x0, blocking collectives: 36.5 us -> none  [shards(): lax.pmax((jnp.max(teacher_logits, axis=1), jnp.max(student_logits, axis=1...]
    ppermute x0 -> x28, starting transfers between devices: none -> 34.4 us  [the longest x24 33.7 us: along(): return lax.ppermute(x, 'section', perm)]
  transfers between devices with their start and end apart: 4 -> 31, of which waited for: 4 -> 22; matrix products, arithmetic and copies ran while one was open for 4% -> 13% of each run, Pallas kernels for 0% -> 0%
where the time goes in v1:
time: 246 us; the launch traced here: 245 us
  waiting for transfers between devices  135 us (55%)
  starting transfers between devices  52.3 us (21%)
  matrix products  23 us (9%)
  other arithmetic  13.5 us (5%)
  blocking collectives  10.7 us (4%)
  local copies, waits for them, and re-layouts  7.73 us (3%)
  between operations  2.77 us (1%)
    ppermute x24, waiting for transfers between devices, along(): return lax.ppermute(x, 'section', perm)  106 us
    ppermute x24, starting transfers between devices, along(): return lax.ppermute(x, 'section', perm)  33.7 us
    all_to_all x2, waiting for transfers between devices, spread(): return lax.all_to_all(jnp.broadcast_to(x[None], (n,) + x.shape), axis, 0, 0)  23.2 us
    all_to_all x2, starting transfers between devices, spread(): return lax.all_to_all(jnp.broadcast_to(x[None], (n,) + x.shape), axis, 0, 0)  13 us
    all_to_all x1, blocking collectives, spread(): return lax.all_to_all(jnp.broadcast_to(x[None], (n,) + x.shape), axis, 0, 0)  10.7 us
    dot_general x2, matrix products, outer(): lax.dot_general(x, g, (((0,), (0,)), ((), ())), preferred_element_type=f32)  7.46 us
    dot_general x2, matrix products, logits_part(): jnp.dot(sib, sib_head, preferred_element_type=f32)  6.32 us
    dot_general x2, matrix products, back(): lax.dot_general(x, student_head, (((1,), (1,)), ((), ())), preferred_elem...  5.23 us
  transfers between devices with their start and end apart: 31, of which 22 were waited for; matrix products, arithmetic and copies ran while one was open for 13% of the time, Pallas kernels for 0%

profile of v1, /device:TPU:2, one launch (start us, length us, event | category | flops | bytes accessed | tf_op | source)
XLA Modules:
  0.0 244.5 jit_solution(16399450682013242733)
XLA Ops:
  3.0 7.5 %all-to-all-start = ((bf16[16,40,768]{2,1,0:T(8,128)(2,1)}), bf16[16,40,768]{2,1,0:T(8,128)(2,1)S(1)}, u32[]{:S(2)}, u32[]{:S(2)}) async-start(bf16[16,40,768]{2,1,0:T(8,128)(2,1)} %broadcast_in_dim.4), calls=%async_computation | async-start | bytes 1966080 | tf_op jit(solution)/shard_map/all_to_all | solution.py:34
  10.5 15.4 %all-to-all-done = bf16[16,40,768]{2,1,0:T(8,128)(2,1)S(1)} async-done(((bf16[16,40,768]{2,1,0:T(8,128)(2,1)}), bf16[16,40,768]{2,1,0:T(8,128)(2,1)S(1)}, u32[]{:S(2)}, u32[]{:S(2)}) %all-to-all-start) | async-done | bytes 983072 | tf_op jit(solution)/shard_map/all_to_all | solution.py:34
  26.4 2.4 fusion.17
  28.8 2.6 %convolution_add_fusion = f32[320,4096]{1,0:T(8,128)S(1)} fusion(f32[320,4096]{1,0:T(8,128)S(1)} %fusion.17, bf16[256,4096]{1,0:T(8,128)(2,1)} %collective-permute-done.10, bf16[320,768]{1,0:T(8,128)(2,1)S(1)} %collective-permute-done), kind=kOutput, calls=%fused_computation | convolution fusion | flops 672399360 | bytes 12746752 | tf_op jit(solution)/shard_map/dot_general | solution.py:55
  31.5 2.0 collective-permute-start.11
  33.5 4.0 %collective-permute-start.15 = (f32[40,2048]{1,0:T(8,128)S(1)}, f32[40,2048]{1,0:T(8,128)S(1)}, u32[]{:S(2)}, u32[]{:S(2)}) collective-permute-start(f32[40,2048]{1,0:T(8,128)S(1)} %get-tuple-element.30), channel_id=1, source_target_pairs={{0,224},{16,240},{32,0},{48,16},{64,32},{80,48},{96,64},{112,80},{... | collective-permute-start | bytes 983048 | tf_op jit(solution)/shard_map/ppermute | solution.py:27
  37.5 1.5 fusion.11
  39.1 6.7 %collective-permute-done.11 = f32[40,2048]{1,0:T(8,128)S(1)} collective-permute-done((f32[40,2048]{1,0:T(8,128)S(1)}, f32[40,2048]{1,0:T(8,128)S(1)}, u32[]{:S(2)}, u32[]{:S(2)}) %collective-permute-start.11) | collective-permute-done | bytes 327712 | tf_op jit(solution)/shard_map/ppermute | solution.py:27
  46.1 3.7 %convolution_add_fusion.1 = f32[320,4096]{1,0:T(8,128)S(1)} fusion(f32[320,4096]{1,0:T(8,128)S(1)} %fusion.11, bf16[512,4096]{1,0:T(8,128)(2,1)} %collective-permute-done.1, bf16[320,768]{1,0:T(8,128)(2,1)S(1)} %collective-permute-done), kind=kOutput, calls=%fused_computation.1 | convolution fusion | flops 1343488000 | bytes 15007744 | tf_op jit(solution)/shard_map/dot_general | solution.py:55
  49.9 2.8 %collective-permute-start.2 = (f32[40,2048]{1,0:T(8,128)S(1)}, f32[40,2048]{1,0:T(8,128)S(1)}, u32[]{:S(2)}, u32[]{:S(2)}) collective-permute-start(f32[40,2048]{1,0:T(8,128)S(1)} %get-tuple-element.39), channel_id=1, source_target_pairs={{0,32},{16,48},{32,64},{48,80},{64,96},{80,112},{96,128},{112,144}... | collective-permute-start | bytes 983048 | tf_op jit(solution)/shard_map/ppermute | solution.py:27
  53.4 2.0 collective-permute-start.16
  55.4 15.5 %collective-permute-done.2 = f32[40,2048]{1,0:T(8,128)S(1)} collective-permute-done((f32[40,2048]{1,0:T(8,128)S(1)}, f32[40,2048]{1,0:T(8,128)S(1)}, u32[]{:S(2)}, u32[]{:S(2)}) %collective-permute-start.2) | collective-permute-done | bytes 327712 | tf_op jit(solution)/shard_map/ppermute | solution.py:27
  71.4 3.3 %collective-permute-start.7 = (f32[40,4096]{1,0:T(8,128)S(1)}, f32[40,4096]{1,0:T(8,128)S(1)}, u32[]{:S(2)}, u32[]{:S(2)}) collective-permute-start(f32[40,4096]{1,0:T(8,128)S(1)} %pad_maximum_fusion.1), channel_id=1, source_target_pairs={{0,224},{16,240},{32,0},{48,16},{64,32},{80,48},{96,64},{112,80},{... | collective-permute-start | bytes 1966088 | tf_op jit(solution)/shard_map/ppermute | solution.py:27
  74.7 3.6 %collective-permute-done.16 = f32[40,4096]{1,0:T(8,128)S(1)} collective-permute-done((f32[40,4096]{1,0:T(8,128)S(1)}, f32[40,4096]{1,0:T(8,128)S(1)}, u32[]{:S(2)}, u32[]{:S(2)}) %collective-permute-start.16) | collective-permute-done | bytes 655392 | tf_op jit(solution)/shard_map/ppermute | solution.py:27
  78.5 2.1 collective-permute-start.13
  80.6 1.2 collective-permute-start.17
  81.8 8.4 %collective-permute-done.3 = f32[40,4096]{1,0:T(8,128)S(1)} collective-permute-done((f32[40,4096]{1,0:T(8,128)S(1)}, f32[40,4096]{1,0:T(8,128)S(1)}, u32[]{:S(2)}, u32[]{:S(2)}) %collective-permute-start.3) | collective-permute-done | bytes 655392 | tf_op jit(solution)/shard_map/ppermute | solution.py:27
  90.2 2.2 collective-permute-done.7
  92.5 2.1 collective-permute-start.4
  94.6 1.2 collective-permute-start.8
  95.8 8.4 %collective-permute-done.13 = f32[40,4096]{1,0:T(8,128)S(1)} collective-permute-done((f32[40,4096]{1,0:T(8,128)S(1)}, f32[40,4096]{1,0:T(8,128)S(1)}, u32[]{:S(2)}, u32[]{:S(2)}) %collective-permute-start.13) | collective-permute-done | bytes 655392 | tf_op jit(solution)/shard_map/ppermute | solution.py:27
  104.3 2.2 collective-permute-done.17
  107.5 1.2 collective-permute-start.18
  109.5 8.8 %collective-permute-done.4 = f32[40,4096]{1,0:T(8,128)S(1)} collective-permute-done((f32[40,4096]{1,0:T(8,128)S(1)}, f32[40,4096]{1,0:T(8,128)S(1)}, u32[]{:S(2)}, u32[]{:S(2)}) %collective-permute-start.4) | collective-permute-done | bytes 655392 | tf_op jit(solution)/shard_map/ppermute | solution.py:27
  118.3 2.2 collective-permute-done.8
  120.5 1.2 slice_add_fusion.7
  123.7 10.8 %collective-permute-done.18 = f32[40,4096]{1,0:T(8,128)S(1)} collective-permute-done((f32[40,4096]{1,0:T(8,128)}, f32[40,4096]{1,0:T(8,128)S(1)}, u32[]{:S(2)}, u32[]{:S(2)}) %collective-permute-start.18) | collective-permute-done | bytes 655392 | tf_op jit(solution)/shard_map/ppermute | solution.py:27
  134.5 1.3 fusion.20
  135.8 10.9 %collective-permute-done.9 = f32[40,4096]{1,0:T(8,128)} collective-permute-done((f32[40,4096]{1,0:T(8,128)}, f32[40,4096]{1,0:T(8,128)}, u32[]{:S(2)}, u32[]{:S(2)}) %collective-permute-start.9) | collective-permute-done | bytes 655392 | tf_op jit(solution)/shard_map/ppermute | solution.py:27
  146.8 1.7 fusion.22
  149.3 10.7 %all_to_all.20 = f32[16,1,320]{2,1,0:T(1,128)S(1)} all-to-all(f32[16,1,320]{2,1,0:T(1,128)S(1)} %reshape.77), channel_id=1, replica_groups=mesh['section'=16,'tensor'=16] {'tensor'}, dimensions={0} | all-to-all | bytes 40960 | tf_op jit(solution)/shard_map/all_to_all | solution.py:34
  161.4 1.2 constant_dynamic-update-slice_fusion.6
  162.7 1.4 collective-permute-start.19
  164.7 6.7 %collective-permute-done.19 = bf16[40,4096]{1,0:T(8,128)(2,1)S(1)} collective-permute-done((bf16[40,4096]{1,0:T(8,128)(2,1)S(1)}, bf16[40,4096]{1,0:T(8,128)(2,1)S(1)}, u32[]{:S(2)}, u32[]{:S(2)}) %collective-permute-start.19) | collective-permute-done | bytes 327712 | tf_op jit(solution)/shard_map/ppermute | solution.py:27
  174.2 7.2 %collective-permute-done.20 = bf16[40,4096]{1,0:T(8,128)(2,1)S(1)} collective-permute-done((bf16[40,4096]{1,0:T(8,128)(2,1)S(1)}, bf16[40,4096]{1,0:T(8,128)(2,1)S(1)}, u32[]{:S(2)}, u32[]{:S(2)}) %collective-permute-start.20) | collective-permute-done | bytes 327712 | tf_op jit(solution)/shard_map/ppermute | solution.py:27
  184.5 5.6 %collective-permute-done.21 = bf16[40,4096]{1,0:T(8,128)(2,1)S(1)} collective-permute-done((bf16[40,4096]{1,0:T(8,128)(2,1)S(1)}, bf16[40,4096]{1,0:T(8,128)(2,1)S(1)}, u32[]{:S(2)}, u32[]{:S(2)}) %collective-permute-start.21) | collective-permute-done | bytes 327712 | tf_op jit(solution)/shard_map/ppermute | solution.py:27
  190.1 2.3 collective-permute-start.26
  193.7 1.8 collective-permute-done.26
  195.5 4.0 %collective-permute-done.25 = bf16[40,2048]{1,0:T(8,128)(2,1)S(1)} collective-permute-done((bf16[40,2048]{1,0:T(8,128)(2,1)S(1)}, bf16[40,2048]{1,0:T(8,128)(2,1)S(1)}, u32[]{:S(2)}, u32[]{:S(2)}) %collective-permute-start.25) | collective-permute-done | bytes 163872 | tf_op jit(solution)/shard_map/ppermute | solution.py:27
  203.1 1.3 broadcast_in_dim_broadcast_in_dim_broadcast_in_dim.3
  204.4 5.6 %all-to-all-start.2 = ((f32[16,8,128]{2,1,0:T(8,128)}), f32[16,8,128]{2,1,0:T(8,128)S(1)}, u32[]{:S(2)}, u32[]{:S(2)}) async-start(f32[16,8,128]{2,1,0:T(8,128)} %broadcast_in_dim_broadcast_in_dim_broadcast_in_dim.3), calls=%async_computation.2 | async-start | bytes 131072 | tf_op jit(solution)/shard_map/all_to_all | solution.py:34
  210.0 7.8 %all-to-all-done.2 = f32[16,8,128]{2,1,0:T(8,128)S(1)} async-done(((f32[16,8,128]{2,1,0:T(8,128)}), f32[16,8,128]{2,1,0:T(8,128)S(1)}, u32[]{:S(2)}, u32[]{:S(2)}) %all-to-all-start.2) | async-done | bytes 65568 | tf_op jit(solution)/shard_map/all_to_all | solution.py:34
  219.1 2.6 %fusion.27 = f32[320,256]{1,0:T(8,128)S(1)} fusion(bf16[320,4096]{1,0:T(8,128)(2,1)} %constant_dynamic-update-slice_fusion, bf16[256,4096]{1,0:T(8,128)(2,1)S(1)} %copy-done.3), kind=kOutput, calls=%fused_computation.75 | convolution fusion | flops 671088640 | bytes 5046272 | tf_op jit(solution)/shard_map/dot_general | solution.py:144
  221.8 2.6 %fusion.28 = f32[320,256]{1,0:T(8,128)S(1)} fusion(bf16[320,4096]{1,0:T(8,128)(2,1)} %collective-permute-done.27, bf16[256,4096]{1,0:T(8,128)(2,1)S(1)} %copy-done.3), kind=kOutput, calls=%fused_computation.76 | convolution fusion | flops 671088640 | bytes 5046272 | tf_op jit(solution)/shard_map/dot_general | solution.py:144
  225.4 4.9 %all-to-all-start.3 = ((f32[16,40,256]{2,1,0:T(8,128)}), f32[16,40,256]{2,1,0:T(8,128)S(1)}, u32[]{:S(2)}, u32[]{:S(2)}) async-start(f32[16,40,256]{2,1,0:T(8,128)} %bitcast.23), calls=%async_computation.3 | async-start | bytes 1310720 | tf_op jit(solution)/shard_map/all_to_all | solution.py:158
  230.3 3.0 %fusion.13 = f32[256,4096]{1,0:T(8,128)S(1)} fusion(bf16[320,4096]{1,0:T(8,128)(2,1)} %collective-permute-done.27, bf16[320,768]{1,0:T(8,128)(2,1)S(1)} %bitcast.51), kind=kOutput, calls=%fused_computation.48 | convolution fusion | flops 671088640 | bytes 6979584 | tf_op jit(solution)/shard_map/dot_general | solution.py:161
  233.3 4.4 %fusion = bf16[256,4096]{1,0:T(8,128)(2,1)} fusion(f32[256,4096]{1,0:T(8,128)S(1)} %fusion.13, bf16[320,4096]{1,0:T(8,128)(2,1)} %constant_dynamic-update-slice_fusion, bf16[320,768]{1,0:T(8,128)(2,1)S(1)} %bitcast.49), kind=kOutput, calls=%fused_computation.3 | convolution fusion | flops 673185792 | bytes 9076736 | tf_op jit(solution)/shard_map/dot_general | solution.py:161
  237.8 5.0 %all-to-all-done.3 = f32[16,40,256]{2,1,0:T(8,128)S(1)} async-done(((f32[16,40,256]{2,1,0:T(8,128)}), f32[16,40,256]{2,1,0:T(8,128)S(1)}, u32[]{:S(2)}, u32[]{:S(2)}) %all-to-all-start.3) | async-done | bytes 655392 | tf_op jit(solution)/shard_map/all_to_all | solution.py:158
  (80 shorter events, 24.6 us)
Async XLA Ops:
  0.6 28.2 %collective-permute-start.10 = (bf16[256,4096]{1,0:T(8,128)(2,1)}, bf16[256,4096]{1,0:T(8,128)(2,1)}, u32[]{:S(2)}, u32[]{:S(2)}) collective-permute-start(bf16[256,4096]{1,0:T(8,128)(2,1)} %param.8), channel_id=1, source_target_pairs={{0,16},{16,0},{32,48},{48,32},{64,80},{80,64},{96,112},{112,96},{1... | collective-permute-start | bytes 6291464 | tf_op jit(solution)/shard_map/ppermute | solution.py:30
  0.7 45.4 %collective-permute-start.1 = (bf16[512,4096]{1,0:T(8,128)(2,1)}, bf16[512,4096]{1,0:T(8,128)(2,1)}, u32[]{:S(2)}, u32[]{:S(2)}) collective-permute-start(bf16[512,4096]{1,0:T(8,128)(2,1)} %param.7), channel_id=1, source_target_pairs={{0,16},{16,0},{32,48},{48,32},{64,80},{80,64},{96,112},{112,96},{1... | collective-permute-start | bytes 12582920 | tf_op jit(solution)/shard_map/ppermute | solution.py:30
  3.0 22.8 %all-to-all-start = ((bf16[16,40,768]{2,1,0:T(8,128)(2,1)}), bf16[16,40,768]{2,1,0:T(8,128)(2,1)S(1)}, u32[]{:S(2)}, u32[]{:S(2)}) async-start(bf16[16,40,768]{2,1,0:T(8,128)(2,1)} %broadcast_in_dim.4), calls=%async_computation | async-start | bytes 1966080 | tf_op jit(solution)/shard_map/all_to_all | solution.py:34
  26.3 2.5 %collective-permute-start = (bf16[320,768]{1,0:T(8,128)(2,1)S(1)}, bf16[320,768]{1,0:T(8,128)(2,1)S(1)}, u32[]{:S(2)}, u32[]{:S(2)}) collective-permute-start(bf16[320,768]{1,0:T(8,128)(2,1)S(1)} %bitcast.50), channel_id=1, source_target_pairs={{0,16},{16,0},{32,48},{48,32},{64,80},{80,64},{96,112},{112,96},{1... | collective-permute-start | bytes 1474568 | tf_op jit(solution)/shard_map/ppermute | solution.py:30
  28.8 8.7 %copy-start.2 = (bf16[512,4096]{1,0:T(8,128)(2,1)S(1)}, bf16[512,4096]{1,0:T(8,128)(2,1)}, u32[]{:S(2)}) copy-start(bf16[512,4096]{1,0:T(8,128)(2,1)} %param.7) | copy-start | bytes 12582916
  31.5 75.0 %copy-start = (f32[320,4096]{1,0:T(8,128)}, f32[320,4096]{1,0:T(8,128)S(1)}, u32[]{:S(2)}) copy-start(f32[320,4096]{1,0:T(8,128)S(1)} %convolution_add_fusion) | copy-start | bytes 15728644
  31.5 14.3 %collective-permute-start.11 = (f32[40,2048]{1,0:T(8,128)S(1)}, f32[40,2048]{1,0:T(8,128)S(1)}, u32[]{:S(2)}, u32[]{:S(2)}) collective-permute-start(f32[40,2048]{1,0:T(8,128)S(1)} %get-tuple-element.29), channel_id=1, source_target_pairs={{0,32},{16,48},{32,64},{48,80},{64,96},{80,112},{96,128},{112,144}... | collective-permute-start | bytes 983048 | tf_op jit(solution)/shard_map/ppermute | solution.py:27
  33.5 12.3 %collective-permute-start.15 = (f32[40,2048]{1,0:T(8,128)S(1)}, f32[40,2048]{1,0:T(8,128)S(1)}, u32[]{:S(2)}, u32[]{:S(2)}) collective-permute-start(f32[40,2048]{1,0:T(8,128)S(1)} %get-tuple-element.30), channel_id=1, source_target_pairs={{0,224},{16,240},{32,0},{48,16},{64,32},{80,48},{96,64},{112,80},{... | collective-permute-start | bytes 983048 | tf_op jit(solution)/shard_map/ppermute | solution.py:27
  46.0 28.7 %collective-permute-start.12 = (f32[40,4096]{1,0:T(8,128)S(1)}, f32[40,4096]{1,0:T(8,128)S(1)}, u32[]{:S(2)}, u32[]{:S(2)}) collective-permute-start(f32[40,4096]{1,0:T(8,128)S(1)} %pad_maximum_fusion.2), channel_id=1, source_target_pairs={{0,32},{16,48},{32,64},{48,80},{64,96},{80,112},{96,128},{112,144}... | collective-permute-start | bytes 1966088 | tf_op jit(solution)/shard_map/ppermute | solution.py:27
  49.9 70.6 %copy-start.1 = (f32[320,4096]{1,0:T(8,128)}, f32[320,4096]{1,0:T(8,128)S(1)}, u32[]{:S(2)}) copy-start(f32[320,4096]{1,0:T(8,128)S(1)} %convolution_add_fusion.1) | copy-start | bytes 15728644
  49.9 21.0 %collective-permute-start.2 = (f32[40,2048]{1,0:T(8,128)S(1)}, f32[40,2048]{1,0:T(8,128)S(1)}, u32[]{:S(2)}, u32[]{:S(2)}) collective-permute-start(f32[40,2048]{1,0:T(8,128)S(1)} %get-tuple-element.39), channel_id=1, source_target_pairs={{0,32},{16,48},{32,64},{48,80},{64,96},{80,112},{96,128},{112,144}... | collective-permute-start | bytes 983048 | tf_op jit(solution)/shard_map/ppermute | solution.py:27
  52.7 18.2 %collective-permute-start.6 = (f32[40,2048]{1,0:T(8,128)S(1)}, f32[40,2048]{1,0:T(8,128)S(1)}, u32[]{:S(2)}, u32[]{:S(2)}) collective-permute-start(f32[40,2048]{1,0:T(8,128)S(1)} %get-tuple-element.40), channel_id=1, source_target_pairs={{0,224},{16,240},{32,0},{48,16},{64,32},{80,48},{96,64},{112,80},{... | collective-permute-start | bytes 983048 | tf_op jit(solution)/shard_map/ppermute | solution.py:27
  53.4 25.0 %collective-permute-start.16 = (f32[40,4096]{1,0:T(8,128)S(1)}, f32[40,4096]{1,0:T(8,128)S(1)}, u32[]{:S(2)}, u32[]{:S(2)}) collective-permute-start(f32[40,4096]{1,0:T(8,128)S(1)} %pad_maximum_fusion.3), channel_id=1, source_target_pairs={{0,224},{16,240},{32,0},{48,16},{64,32},{80,48},{96,64},{112,80},{... | collective-permute-start | bytes 1966088 | tf_op jit(solution)/shard_map/ppermute | solution.py:27
  71.1 19.1 %collective-permute-start.3 = (f32[40,4096]{1,0:T(8,128)S(1)}, f32[40,4096]{1,0:T(8,128)S(1)}, u32[]{:S(2)}, u32[]{:S(2)}) collective-permute-start(f32[40,4096]{1,0:T(8,128)S(1)} %pad_maximum_fusion), channel_id=1, source_target_pairs={{0,32},{16,48},{32,64},{48,80},{64,96},{80,112},{96,128},{112,144}... | collective-permute-start | bytes 1966088 | tf_op jit(solution)/shard_map/ppermute | solution.py:27
  71.4 21.0 %collective-permute-start.7 = (f32[40,4096]{1,0:T(8,128)S(1)}, f32[40,4096]{1,0:T(8,128)S(1)}, u32[]{:S(2)}, u32[]{:S(2)}) collective-permute-start(f32[40,4096]{1,0:T(8,128)S(1)} %pad_maximum_fusion.1), channel_id=1, source_target_pairs={{0,224},{16,240},{32,0},{48,16},{64,32},{80,48},{96,64},{112,80},{... | collective-permute-start | bytes 1966088 | tf_op jit(solution)/shard_map/ppermute | solution.py:27
  78.5 25.8 %collective-permute-start.13 = (f32[40,4096]{1,0:T(8,128)S(1)}, f32[40,4096]{1,0:T(8,128)S(1)}, u32[]{:S(2)}, u32[]{:S(2)}) collective-permute-start(f32[40,4096]{1,0:T(8,128)S(1)} %get-tuple-element.23), channel_id=1, source_target_pairs={{0,32},{16,48},{32,64},{48,80},{64,96},{80,112},{96,128},{112,144}... | collective-permute-start | bytes 1966088 | tf_op jit(solution)/shard_map/ppermute | solution.py:27
  80.6 25.8 %collective-permute-start.17 = (f32[40,4096]{1,0:T(8,128)S(1)}, f32[40,4096]{1,0:T(8,128)S(1)}, u32[]{:S(2)}, u32[]{:S(2)}) collective-permute-start(f32[40,4096]{1,0:T(8,128)S(1)} %get-tuple-element.24), channel_id=1, source_target_pairs={{0,224},{16,240},{32,0},{48,16},{64,32},{80,48},{96,64},{112,80},{... | collective-permute-start | bytes 1966088 | tf_op jit(solution)/shard_map/ppermute | solution.py:27
  92.5 25.8 %collective-permute-start.4 = (f32[40,4096]{1,0:T(8,128)S(1)}, f32[40,4096]{1,0:T(8,128)S(1)}, u32[]{:S(2)}, u32[]{:S(2)}) collective-permute-start(f32[40,4096]{1,0:T(8,128)S(1)} %get-tuple-element.33), channel_id=1, source_target_pairs={{0,32},{16,48},{32,64},{48,80},{64,96},{80,112},{96,128},{112,144}... | collective-permute-start | bytes 1966088 | tf_op jit(solution)/shard_map/ppermute | solution.py:27
  94.6 25.8 %collective-permute-start.8 = (f32[40,4096]{1,0:T(8,128)S(1)}, f32[40,4096]{1,0:T(8,128)S(1)}, u32[]{:S(2)}, u32[]{:S(2)}) collective-permute-start(f32[40,4096]{1,0:T(8,128)S(1)} %get-tuple-element.34), channel_id=1, source_target_pairs={{0,224},{16,240},{32,0},{48,16},{64,32},{80,48},{96,64},{112,80},{... | collective-permute-start | bytes 1966088 | tf_op jit(solution)/shard_map/ppermute | solution.py:27
  107.5 27.1 %collective-permute-start.18 = (f32[40,4096]{1,0:T(8,128)}, f32[40,4096]{1,0:T(8,128)S(1)}, u32[]{:S(2)}, u32[]{:S(2)}) collective-permute-start(f32[40,4096]{1,0:T(8,128)} %get-tuple-element.22), channel_id=1, source_target_pairs={{0,224},{16,240},{32,0},{48,16},{64,32},{80,48},{96,64},{112,80},{... | collective-permute-start | bytes 1966088 | tf_op jit(solution)/shard_map/ppermute | solution.py:27
  108.6 25.9 %collective-permute-start.14 = (f32[40,4096]{1,0:T(8,128)S(1)}, f32[40,4096]{1,0:T(8,128)S(1)}, u32[]{:S(2)}, u32[]{:S(2)}) collective-permute-start(f32[40,4096]{1,0:T(8,128)S(1)} %get-tuple-element.21), channel_id=1, source_target_pairs={{0,32},{16,48},{32,64},{48,80},{64,96},{80,112},{96,128},{112,144}... | collective-permute-start | bytes 1966088 | tf_op jit(solution)/shard_map/ppermute | solution.py:27
  121.7 25.0 %collective-permute-start.9 = (f32[40,4096]{1,0:T(8,128)}, f32[40,4096]{1,0:T(8,128)}, u32[]{:S(2)}, u32[]{:S(2)}) collective-permute-start(f32[40,4096]{1,0:T(8,128)} %get-tuple-element.32), channel_id=1, source_target_pairs={{0,224},{16,240},{32,0},{48,16},{64,32},{80,48},{96,64},{112,80},{... | collective-permute-start | bytes 1966088 | tf_op jit(solution)/shard_map/ppermute | solution.py:27
  122.9 23.9 %collective-permute-start.5 = (f32[40,4096]{1,0:T(8,128)}, f32[40,4096]{1,0:T(8,128)}, u32[]{:S(2)}, u32[]{:S(2)}) collective-permute-start(f32[40,4096]{1,0:T(8,128)} %get-tuple-element.31), channel_id=1, source_target_pairs={{0,32},{16,48},{32,64},{48,80},{64,96},{80,112},{96,128},{112,144}... | collective-permute-start | bytes 1966088 | tf_op jit(solution)/shard_map/ppermute | solution.py:27
  123.7 24.7 %copy-start.4 = (s32[40]{0:T(128)S(1)}, s32[40]{0:T(128)}, u32[]{:S(2)}) copy-start(s32[40]{0:T(128)} %param.9) | copy-start | bytes 484
  162.7 8.8 %collective-permute-start.19 = (bf16[40,4096]{1,0:T(8,128)(2,1)S(1)}, bf16[40,4096]{1,0:T(8,128)(2,1)S(1)}, u32[]{:S(2)}, u32[]{:S(2)}) collective-permute-start(bf16[40,4096]{1,0:T(8,128)(2,1)S(1)} %get-tuple-element.16), channel_id=1, source_target_pairs={{0,224},{16,240},{32,0},{48,16},{64,32},{80,48},{96,64},{112,80},{... | collective-permute-start | bytes 983048 | tf_op jit(solution)/shard_map/ppermute | solution.py:27
  164.1 8.8 %collective-permute-start.22 = (bf16[40,4096]{1,0:T(8,128)(2,1)S(1)}, bf16[40,4096]{1,0:T(8,128)(2,1)S(1)}, u32[]{:S(2)}, u32[]{:S(2)}) collective-permute-start(bf16[40,4096]{1,0:T(8,128)(2,1)S(1)} %get-tuple-element.16), channel_id=1, source_target_pairs={{0,32},{16,48},{32,64},{48,80},{64,96},{80,112},{96,128},{112,144}... | collective-permute-start | bytes 983048 | tf_op jit(solution)/shard_map/ppermute | solution.py:27
  171.4 10.0 %collective-permute-start.20 = (bf16[40,4096]{1,0:T(8,128)(2,1)S(1)}, bf16[40,4096]{1,0:T(8,128)(2,1)S(1)}, u32[]{:S(2)}, u32[]{:S(2)}) collective-permute-start(bf16[40,4096]{1,0:T(8,128)(2,1)S(1)} %collective-permute-done.19), channel_id=1, source_target_pairs={{0,224},{16,240},{32,0},{48,16},{64,32},{80,48},{96,64},{112,80},{... | collective-permute-start | bytes 983048 | tf_op jit(solution)/shard_map/ppermute | solution.py:27
  172.9 9.9 %collective-permute-start.23 = (bf16[40,4096]{1,0:T(8,128)(2,1)S(1)}, bf16[40,4096]{1,0:T(8,128)(2,1)S(1)}, u32[]{:S(2)}, u32[]{:S(2)}) collective-permute-start(bf16[40,4096]{1,0:T(8,128)(2,1)S(1)} %collective-permute-done.22), channel_id=1, source_target_pairs={{0,32},{16,48},{32,64},{48,80},{64,96},{80,112},{96,128},{112,144}... | collective-permute-start | bytes 983048 | tf_op jit(solution)/shard_map/ppermute | solution.py:27
  173.5 45.7 %copy-start.3 = (bf16[256,4096]{1,0:T(8,128)(2,1)S(1)}, bf16[256,4096]{1,0:T(8,128)(2,1)}, u32[]{:S(2)}) copy-start(bf16[256,4096]{1,0:T(8,128)(2,1)} %param.8) | copy-start | bytes 6291460
  181.4 8.7 %collective-permute-start.21 = (bf16[40,4096]{1,0:T(8,128)(2,1)S(1)}, bf16[40,4096]{1,0:T(8,128)(2,1)S(1)}, u32[]{:S(2)}, u32[]{:S(2)}) collective-permute-start(bf16[40,4096]{1,0:T(8,128)(2,1)S(1)} %collective-permute-done.20), channel_id=1, source_target_pairs={{0,224},{16,240},{32,0},{48,16},{64,32},{80,48},{96,64},{112,80},{... | collective-permute-start | bytes 983048 | tf_op jit(solution)/shard_map/ppermute | solution.py:27
  182.8 10.0 %collective-permute-start.24 = (bf16[40,4096]{1,0:T(8,128)(2,1)S(1)}, bf16[40,4096]{1,0:T(8,128)(2,1)S(1)}, u32[]{:S(2)}, u32[]{:S(2)}) collective-permute-start(bf16[40,4096]{1,0:T(8,128)(2,1)S(1)} %collective-permute-done.23), channel_id=1, source_target_pairs={{0,32},{16,48},{32,64},{48,80},{64,96},{80,112},{96,128},{112,144}... | collective-permute-start | bytes 983048 | tf_op jit(solution)/shard_map/ppermute | solution.py:27
  190.1 5.4 %collective-permute-start.26 = (bf16[40,2048]{1,0:T(8,128)(2,1)S(1)}, bf16[40,2048]{1,0:T(8,128)(2,1)S(1)}, u32[]{:S(2)}, u32[]{:S(2)}) collective-permute-start(bf16[40,2048]{1,0:T(8,128)(2,1)S(1)} %slice.223), channel_id=1, source_target_pairs={{0,224},{16,240},{32,0},{48,16},{64,32},{80,48},{96,64},{112,80},{... | collective-permute-start | bytes 491528 | tf_op jit(solution)/shard_map/ppermute | solution.py:27
  192.9 6.6 %collective-permute-start.25 = (bf16[40,2048]{1,0:T(8,128)(2,1)S(1)}, bf16[40,2048]{1,0:T(8,128)(2,1)S(1)}, u32[]{:S(2)}, u32[]{:S(2)}) collective-permute-start(bf16[40,2048]{1,0:T(8,128)(2,1)S(1)} %slice.222), channel_id=1, source_target_pairs={{0,32},{16,48},{32,64},{48,80},{64,96},{80,112},{96,128},{112,144}... | collective-permute-start | bytes 491528 | tf_op jit(solution)/shard_map/ppermute | solution.py:27
  202.5 19.3 %collective-permute-start.27 = (bf16[320,4096]{1,0:T(8,128)(2,1)}, bf16[320,4096]{1,0:T(8,128)(2,1)}, u32[]{:S(2)}, u32[]{:S(2)}) collective-permute-start(bf16[320,4096]{1,0:T(8,128)(2,1)} %constant_dynamic-update-slice_fusion), channel_id=1, source_target_pairs={{0,16},{16,0},{32,48},{48,32},{64,80},{80,64},{96,112},{112,96},{1... | collective-permute-start | bytes 7864328 | tf_op jit(solution)/shard_map/ppermute | solution.py:30
  204.4 13.4 %all-to-all-start.2 = ((f32[16,8,128]{2,1,0:T(8,128)}), f32[16,8,128]{2,1,0:T(8,128)S(1)}, u32[]{:S(2)}, u32[]{:S(2)}) async-start(f32[16,8,128]{2,1,0:T(8,128)} %broadcast_in_dim_broadcast_in_dim_broadcast_in_dim.3), calls=%async_computation.2 | async-start | bytes 131072 | tf_op jit(solution)/shard_map/all_to_all | solution.py:34
  225.4 17.3 %all-to-all-start.3 = ((f32[16,40,256]{2,1,0:T(8,128)}), f32[16,40,256]{2,1,0:T(8,128)S(1)}, u32[]{:S(2)}, u32[]{:S(2)}) async-start(f32[16,40,256]{2,1,0:T(8,128)} %bitcast.23), calls=%async_computation.3 | async-start | bytes 1310720 | tf_op jit(solution)/shard_map/all_to_all | solution.py:158
